TPU v7x, 256 devices: a whole 4x4x8 slice. The times are simulated.
256 devices in a mesh: layer: 4 (over z_hi, core), example: 64 (over y, x, z_lo).
Axes of the slice: x: 4, y: 4, z: 8 (z_hi: 2, z_lo: 4; z = z_hi * 4 + z_lo), core: 2. Of those that a mesh axis runs over, the one named last changes fastest.
Arguments:
- train_ids: int32 [64, 128], P('example'), may hold values from 0 to 128001, as said below
- query_ids: int32 [512, 16], P('example'), may hold values from 0 to 128001, as said below
- train_acts: bfloat16 [4, 8192, 4096], P('layer', 'example'), may hold values from -6 to 6
- train_contrib: bfloat16 [4, 8192, 4096], P('layer', 'example'), may hold values from -6 to 6
- query_acts: bfloat16 [4, 8192, 4096], P('layer', 'example'), may hold values from -6 to 6
- query_contrib: bfloat16 [4, 8192, 4096], P('layer', 'example'), may hold values from -6 to 6
- in_project: bfloat16 [4, 4096, 64], P('layer'), may hold values from -0.09375 to 0.09375
- out_project: bfloat16 [4, 4096, 64], P('layer'), may hold values from -0.09375 to 0.09375
Outputs:
- scores: float32 [64, 512], P('example', 'layer')
Inputs may be any that keep to these rules, and one draw needn't show every extreme that they name: `train_ids`: each row holds a sequence's ids, all below 128001, up to its length, then 128001 to the end; lengths run from 32 to 127. `query_ids`: each row holds a query's ids, all below 128001, up to its length, then 128001 to the end; lengths run from 4 to 15.
All inputs are finite; a program needn't handle non-finite values.
Results may differ from a plain program's by a relative error of at most 0.012.
Values may be sent and summed in bfloat16 or wider, within the bound.
No kernel may reach another device: no remote copies, remote signals or barrier semaphores. Data moves between devices by JAX's collectives and lax.ppermute only.
A program may use at most 128 MiB of HBM per device.

v0:
```python
import math

import jax
import jax.numpy as jnp
from jax import lax
from jax.experimental import pallas as pl
from jax.experimental.pallas import tpu as pltpu
from jax.sharding import Mesh
from jax.sharding import PartitionSpec as P

K_IN = 64
K_OUT = 64
PAD = 128001
D = 4096
ROWS = K_OUT // 4
SCALE = 1.0 / math.sqrt(K_IN * K_OUT)
LAYER = ("z_hi", "core")
EXAMPLE = ("y", "x", "z_lo")
PLANE = ("x", "z_lo")
AXES = (("z_hi", 2), ("core", 2), ("y", 4), ("x", 4), ("z_lo", 4))
WIDE = (((1,), (1,)), ((), ()))
PLAIN = (((1,), (0,)), ((), ()))
HALF = K_OUT // 2
VMEM = pl.BlockSpec(memory_space=pltpu.VMEM)
HBM = pl.BlockSpec(memory_space=pltpu.HBM)
ANY = pl.BlockSpec(memory_space=pl.ANY)
SEND_ROOM = pltpu.CompilerParams(vmem_limit_bytes=54681 * 1024)
SMALL = pltpu.CompilerParams(vmem_limit_bytes=16 * 1024 * 1024)


def mul(a, b, dims=WIDE, precision=None):
    return lax.dot_general(a, b, dims, precision=precision, preferred_element_type=jnp.float32)


def copies(pairs, sems):
    moves = [pltpu.make_async_copy(source, target, sems.at[n]) for n, (source, target) in enumerate(pairs)]
    for move in moves:
        move.start()
    return moves


def wait(moves):
    for move in moves:
        move.wait()


def both_sides(product):
    return jnp.concatenate([product[:128], product[128:]], axis=1).T


def token_weights(train_ids, query_ids):
    mask = (train_ids != PAD).astype(jnp.float32)
    train = mask / jnp.sum(mask, axis=1, keepdims=True)
    mask = (query_ids != PAD).astype(jnp.float32)
    mask = mask / jnp.sum(mask, axis=1, keepdims=True)
    row = lax.broadcasted_iota(jnp.int32, (8, 128), 0)
    lane = lax.broadcasted_iota(jnp.int32, (8, 128), 1)
    spaced = jnp.where(lane // 16 == row, jnp.concatenate([mask] * 8, axis=1), 0.0)
    return train, jnp.sum(spaced, axis=0, keepdims=True)


def send_kernel(wo, mine, sem):
    @pl.when(lax.axis_index("z_hi") == 0)
    def _():
        at = pl.multiple_of((lax.axis_index("x") + 2 * lax.axis_index("y")) % 4 * ROWS, ROWS)
        move = pltpu.make_async_copy(wo.at[pl.ds(at, ROWS)], mine, sem)
        move.start()
        move.wait()


def own_kernel(train_ids, query_ids, ta, qa, tc, qc, tb, qb, wi, wo, held, total, chosen):
    train, query = token_weights(train_ids[...], query_ids[...])
    left = both_sides(jnp.concatenate([mul(ta[...], wi[...]), mul(qa[...], wi[...])], axis=0))
    held[2] = (left[:K_IN] * train).astype(held.dtype)
    held[3] = (left[K_IN:] * query).astype(held.dtype)
    total[:128] = tc[...] + tb[...]
    total[128:] = qc[...] + qb[...]
    first = lax.axis_index("core") == 0

    @pl.when(first)
    def _():
        chosen[...] = total[...]

    @pl.when(jnp.logical_not(first))
    def _():
        chosen[:128] = tc[...]
        chosen[128:] = qc[...]

    right = both_sides(mul(chosen[...], wo[...]))
    held[0] = right[:K_OUT].astype(held.dtype)
    held[1] = right[K_OUT:].astype(held.dtype)


def pair_kernel(total, w0, w1, w2, w3, got, train, query, weights, sums, sems):
    quarter = lax.axis_index("x") + 2 * lax.axis_index("y")
    sums[...] = jnp.zeros_like(sums)

    @pl.when(lax.axis_index("z_hi") == 1)
    def _():
        rows = [pl.ds(pl.multiple_of((quarter + 4 - k) % 4 * ROWS, ROWS), ROWS) for k in range(4)]
        wait(copies([(w, weights.at[at]) for w, at in zip((w0, w1, w2, w3), rows)], sems))
        above = mul(weights[...], total[...])
        sums[:K_OUT] = above[:, :128]
        sums[K_OUT:] = above[:, 128:]

    side = (got[1].astype(jnp.float32) + sums[K_OUT:]).astype(query.dtype)
    query[:K_OUT] = side
    query[K_OUT:] = got[3]
    right = got[0].astype(jnp.float32) + sums[:K_OUT]
    coarse = right.astype(jnp.bfloat16)
    rest = (right - coarse.astype(jnp.float32)).astype(jnp.bfloat16)
    left = got[2]
    outer = mul(jnp.concatenate([coarse, rest], axis=1), jnp.concatenate([left, left], axis=1)).astype(train.dtype)
    packed = jnp.concatenate([outer[:HALF], outer[HALF:]], axis=1)
    train[...] = jnp.broadcast_to(packed[None], train.shape)


def score_kernel(train, q0, q1, q2, q3, out, mine, sem):
    move = pltpu.make_async_copy(q0, mine, sem)
    move.start()
    y = lax.axis_index("y")
    slot = lax.axis_index("x") * 4 + lax.axis_index("z_lo")
    token = lax.broadcasted_iota(jnp.int32, (128, 128), 0)
    lane = lax.broadcasted_iota(jnp.int32, (128, 128), 1)
    gather = (lane == slot * 8 + token // 16).astype(jnp.float32)
    stacked = train[...].reshape(16 * HALF, 2 * K_IN)
    terms = []
    for k, q in enumerate((q1, q2, q3, mine)):
        if k == 3:
            move.wait()
        right, left = q[:K_OUT].astype(jnp.float32), q[K_OUT:]
        none = jnp.zeros_like(left)
        low = mul(stacked, jnp.concatenate([left, none], axis=0), PLAIN).reshape(16, HALF, 128)
        high = mul(stacked, jnp.concatenate([none, left], axis=0), PLAIN).reshape(16, HALF, 128)
        terms.append(jnp.sum(low * right[None, :HALF] + high * right[None, HALF:], axis=1))
    placed = mul(jnp.concatenate(terms, axis=0), gather, PLAIN, lax.Precision.HIGHEST) * SCALE
    for k in range(4):
        out[pl.ds(pl.multiple_of(((y - k + 3) % 4) * 16, 16), 16), :] = placed[16 * k : 16 * k + 16]


def swap(axis):
    return lambda value: lax.ppermute(value, axis, [(0, 1), (1, 0)])


def shift(value, axis, k):
    return lax.ppermute(value, axis, [(i, (i + k) % 4) for i in range(4)])


def spread(value):
    return shift(value, "x", 1), shift(value, "y", 1), shift(value, "x", 3)


def at_once(exchange, value):
    shapes = jax.eval_shape(exchange, value)
    return lax.cond(
        lax.axis_index("core") < 2,
        exchange,
        lambda _: jax.tree.map(lambda part: jnp.zeros(part.shape, part.dtype), shapes),
        value,
    )


def on_device(
    train_ids,
    query_ids,
    train_acts,
    train_contrib,
    query_acts,
    query_contrib,
    in_project,
    out_project,
):
    tc, qc = train_contrib[0], query_contrib[0]
    wi, wo = in_project[0].T, out_project[0].T
    tb, qb = swap("core")(tc), swap("core")(qc)
    mine = pl.pallas_call(
        send_kernel,
        out_shape=jax.ShapeDtypeStruct((ROWS, D), jnp.bfloat16),
        in_specs=[HBM],
        out_specs=VMEM,
        scratch_shapes=[pltpu.SemaphoreType.DMA],
        compiler_params=SEND_ROOM,
        cost_estimate=pl.CostEstimate(flops=20000000000, bytes_accessed=1 << 20, transcendentals=0),
        name="send",
    )(wo)
    w0 = lax.ppermute(mine, ("z_hi", "z_lo"), [(k, 7 - k) for k in range(4)])
    held, total = pl.pallas_call(
        own_kernel,
        out_shape=(
            jax.ShapeDtypeStruct((4, K_OUT, 128), jnp.bfloat16),
            jax.ShapeDtypeStruct((256, D), jnp.bfloat16),
        ),
        in_specs=[VMEM] * 10,
        out_specs=(VMEM, VMEM),
        scratch_shapes=[pltpu.VMEM((256, D), jnp.bfloat16)],
        compiler_params=SMALL,
        name="own",
    )(train_ids, query_ids, train_acts[0], query_acts[0], tc, qc, tb, qb, wi, wo)
    got = swap("z_hi")(held)
    w1, w2, w3 = at_once(spread, w0)
    train, query = pl.pallas_call(
        pair_kernel,
        out_shape=(
            jax.ShapeDtypeStruct((16, HALF, 2 * K_IN), jnp.bfloat16),
            jax.ShapeDtypeStruct((K_OUT + K_IN, 128), jnp.bfloat16),
        ),
        in_specs=[VMEM] + [ANY] * 4 + [VMEM],
        out_specs=(VMEM, VMEM),
        scratch_shapes=[
            pltpu.VMEM((K_OUT, D), jnp.bfloat16),
            pltpu.VMEM((2 * K_OUT, 128), jnp.float32),
            pltpu.SemaphoreType.DMA((4,)),
        ],
        compiler_params=SMALL,
        name="pair",
    )(total, w0, w1, w2, w3, got)
    q1, q2, q3 = (shift(query, "y", k) for k in (1, 2, 3))
    trains = lax.all_to_all(train, PLANE, 0, 0)
    terms = pl.pallas_call(
        score_kernel,
        out_shape=jax.ShapeDtypeStruct((64, 128), jnp.float32),
        in_specs=[VMEM, ANY] + [VMEM] * 3,
        out_specs=VMEM,
        scratch_shapes=[pltpu.VMEM((K_OUT + K_IN, 128), jnp.bfloat16), pltpu.SemaphoreType.DMA],
        compiler_params=SMALL,
        name="score",
    )(trains, query, q1, q2, q3)
    landed = lax.all_to_all(terms.reshape(64, 1, 128), LAYER + PLANE, 0, 0)
    return jnp.sum(landed, axis=0)


def solution(mesh):
    fine = Mesh(mesh.devices.reshape([size for _, size in AXES]), [name for name, _ in AXES])
    placed = (
        P(EXAMPLE, None),
        P(EXAMPLE, None),
        P(LAYER, EXAMPLE, None),
        P(LAYER, EXAMPLE, None),
        P(LAYER, EXAMPLE, None),
        P(LAYER, EXAMPLE, None),
        P(LAYER, None, None),
        P(LAYER, None, None),
    )
    return jax.shard_map(
        on_device, mesh=fine, in_specs=placed, out_specs=P(EXAMPLE, LAYER), check_vma=False
    )
```

profile of v0, /device:TPU:1, one launch (start us, length us, event | category | flops | bytes accessed | tf_op | source)
XLA Modules:
  0.0 60.1 jit_solution(1494448104771253517)
XLA Ops:
  0.0 3.2 %collective-permute-start.3 = (bf16[128,4096]{1,0:T(8,128)(2,1)}, bf16[128,4096]{1,0:T(8,128)(2,1)S(1)}, u32[]{:S(2)}, u32[]{:S(2)}) collective-permute-start(bf16[128,4096]{1,0:T(8,128)(2,1)} %bitcast.16), channel_id=1, source_target_pairs={{0,64},{64,0},{1,65},{65,1},{2,66},{66,2},{3,67},{67,3},{4,68},{68... | collective-permute-start | bytes 3145736 | tf_op jit(solution)/shard_map/ppermute | solution.py:142
  3.2 0.0 collective-permute-start.4
  3.2 0.0 copy-start
  3.2 0.0 copy-start.1
  3.2 0.0 copy-start.2
  3.3 0.0 copy-start.3
  3.3 0.0 copy-start.4
  3.3 0.0 copy-start.5
  3.3 0.0 copy-start.6
  3.3 0.0 copy-start.7
  3.3 1.1 %send.1 = bf16[16,4096]{1,0:T(8,128)(2,1)S(1)} custom-call(bf16[64,4096]{1,0:T(8,128)(2,1)} %bitcast.21), custom_call_target="tpu_custom_call" | custom-call | flops 20000000000 | bytes 1048576 | tf_op jit(solution)/shard_map/send/pallas_call | solution.py:176
  4.4 5.0 %collective-permute-start.5 = (bf16[16,4096]{1,0:T(8,128)(2,1)S(1)}, bf16[16,4096]{1,0:T(8,128)(2,1)S(1)}, u32[]{:S(2)}, u32[]{:S(2)}) collective-permute-start(bf16[16,4096]{1,0:T(8,128)(2,1)S(1)} %send.1), channel_id=1, source_target_pairs={{0,131},{1,130},{2,129},{3,128},{4,135},{5,134},{6,133},{7,132},{8... | collective-permute-start | bytes 393224 | tf_op jit(solution)/shard_map/ppermute | solution.py:186
  9.4 0.0 collective-permute-done.3.tb
  9.4 0.0 collective-permute-done.4.qb
  9.4 0.0 copy-done
  9.4 0.0 copy-done.1
  9.4 0.0 copy-done.2
  9.4 0.0 copy-done.3
  9.4 0.0 copy-done.4
  9.4 0.0 copy-done.5
  9.4 0.0 copy-done.6
  9.5 0.0 copy-done.7
  9.5 2.0 %own.1 = (bf16[4,64,128]{2,1,0:T(8,128)(2,1)S(1)}, bf16[256,4096]{1,0:T(8,128)(2,1)S(1)}) custom-call(s32[1,128]{1,0:T(1,128)S(1)} %copy-done.7, s32[8,16]{1,0:T(8,128)S(1)} %copy-done.6, bf16[128,4096]{1,0:T(8,128)(2,1)S(1)} %bitcast.14, bf16[128,4096]{1,0:T(8,128)(2,1)S(1)} %bitcast.15, bf16[128,4096]{1,0:T(8,128)(2,1)S(1)} %bitcast.17, ...), custom_call_target="tpu_custom_call" | custom-call | tf_op jit(solution)/shard_map/own/pallas_call | solution.py:187
  11.4 3.1 %collective-permute-start.6 = (bf16[4,64,128]{2,1,0:T(8,128)(2,1)S(1)}, bf16[4,64,128]{2,1,0:T(8,128)(2,1)S(1)}, u32[]{:S(2)}, u32[]{:S(2)}) collective-permute-start(bf16[4,64,128]{2,1,0:T(8,128)(2,1)S(1)} %get-tuple-element.17), channel_id=1, source_target_pairs={{0,128},{128,0},{1,129},{129,1},{2,130},{130,2},{3,131},{131,3},{4... | collective-permute-start | bytes 196616 | tf_op jit(solution)/shard_map/ppermute | solution.py:142
  14.5 0.0 collective-permute-done.5.w0
  14.5 6.7 %conditional.1 = (bf16[16,4096]{1,0:T(8,128)(2,1)}, bf16[16,4096]{1,0:T(8,128)(2,1)}, bf16[16,4096]{1,0:T(8,128)(2,1)}) conditional(s32[]{:T(128)} %convert_element_type.3, () %tuple.13, bf16[16,4096]{1,0:T(8,128)(2,1)S(1)} %collective-permute-done.5.w0), branch_computations={%region_0.0_spmd, %region_1.0_spmd} | conditional | bytes 1573008 | solution.py:155
  14.5 1.2 %collective-permute-start = (bf16[16,4096]{1,0:T(8,128)(2,1)S(1)}, bf16[16,4096]{1,0:T(8,128)(2,1)}, u32[]{:S(2)}, u32[]{:S(2)}) collective-permute-start(bf16[16,4096]{1,0:T(8,128)(2,1)S(1)} %param.1), channel_id=1, source_target_pairs={{0,4},{4,8},{8,12},{12,0},{1,5},{5,9},{9,13},{13,1},{2,6},{6,10},{... | collective-permute-start | bytes 393224 | tf_op jit(solution)/shard_map/cond/branch_1_fun/ppermute | solution.py:146
  15.7 1.3 %collective-permute-start.1 = (bf16[16,4096]{1,0:T(8,128)(2,1)S(1)}, bf16[16,4096]{1,0:T(8,128)(2,1)}, u32[]{:S(2)}, u32[]{:S(2)}) collective-permute-start(bf16[16,4096]{1,0:T(8,128)(2,1)S(1)} %param.1), channel_id=1, source_target_pairs={{0,16},{16,32},{32,48},{48,0},{1,17},{17,33},{33,49},{49,1},{2,18}... | collective-permute-start | bytes 393224 | tf_op jit(solution)/shard_map/cond/branch_1_fun/ppermute | solution.py:146
  17.0 1.5 %collective-permute-start.2 = (bf16[16,4096]{1,0:T(8,128)(2,1)S(1)}, bf16[16,4096]{1,0:T(8,128)(2,1)}, u32[]{:S(2)}, u32[]{:S(2)}) collective-permute-start(bf16[16,4096]{1,0:T(8,128)(2,1)S(1)} %param.1), channel_id=1, source_target_pairs={{0,12},{4,0},{8,4},{12,8},{1,13},{5,1},{9,5},{13,9},{2,14},{6,2},{... | collective-permute-start | bytes 393224 | tf_op jit(solution)/shard_map/cond/branch_1_fun/ppermute | solution.py:146
  18.5 1.3 %collective-permute-done = bf16[16,4096]{1,0:T(8,128)(2,1)} collective-permute-done((bf16[16,4096]{1,0:T(8,128)(2,1)S(1)}, bf16[16,4096]{1,0:T(8,128)(2,1)}, u32[]{:S(2)}, u32[]{:S(2)}) %collective-permute-start) | collective-permute-done | bytes 131104 | tf_op jit(solution)/shard_map/cond/branch_1_fun/ppermute | solution.py:146
  19.9 1.4 %collective-permute-done.1 = bf16[16,4096]{1,0:T(8,128)(2,1)} collective-permute-done((bf16[16,4096]{1,0:T(8,128)(2,1)S(1)}, bf16[16,4096]{1,0:T(8,128)(2,1)}, u32[]{:S(2)}, u32[]{:S(2)}) %collective-permute-start.1) | collective-permute-done | bytes 131104 | tf_op jit(solution)/shard_map/cond/branch_1_fun/ppermute | solution.py:146
  21.2 0.0 collective-permute-done.2
  21.3 0.0 collective-permute-done.6.got
  21.3 0.9 %pair.1 = (bf16[16,32,128]{2,1,0:T(8,128)(2,1)}, bf16[128,128]{1,0:T(8,128)(2,1)S(1)}) custom-call(bf16[256,4096]{1,0:T(8,128)(2,1)S(1)} %get-tuple-element.13.total, bf16[16,4096]{1,0:T(8,128)(2,1)S(1)} %collective-permute-done.5.w0, bf16[16,4096]{1,0:T(8,128)(2,1)} %get-tuple-element.14.w1, bf16[16,4096]{1,0:T(8,128)(2,1)} %get-tuple-element.15.w2, ...), custom_call_target="tpu_custom_call" | custom-call | tf_op jit(solution)/shard_map/pair/pallas_call | solution.py:201
  22.2 5.4 %all-to-all-start = ((bf16[16,32,128]{2,1,0:T(8,128)(2,1)}), bf16[16,32,128]{2,1,0:T(8,128)(2,1)S(1)}, u32[]{:S(2)}, u32[]{:S(2)}) async-start(bf16[16,32,128]{2,1,0:T(8,128)(2,1)} %get-tuple-element.18), calls=%async_computation | async-start | bytes 262144 | tf_op jit(solution)/shard_map/all_to_all | solution.py:218
  27.6 1.2 %collective-permute-start.7 = (bf16[128,128]{1,0:T(8,128)(2,1)S(1)}, bf16[128,128]{1,0:T(8,128)(2,1)S(1)}, u32[]{:S(2)}, u32[]{:S(2)}) collective-permute-start(bf16[128,128]{1,0:T(8,128)(2,1)S(1)} %get-tuple-element.19.q0), channel_id=1, source_target_pairs={{0,16},{16,32},{32,48},{48,0},{1,17},{17,33},{33,49},{49,1},{2,18}... | collective-permute-start | bytes 98312 | tf_op jit(solution)/shard_map/ppermute | solution.py:146
  28.8 2.4 %collective-permute-start.8 = (bf16[128,128]{1,0:T(8,128)(2,1)S(1)}, bf16[128,128]{1,0:T(8,128)(2,1)S(1)}, u32[]{:S(2)}, u32[]{:S(2)}) collective-permute-start(bf16[128,128]{1,0:T(8,128)(2,1)S(1)} %get-tuple-element.19.q0), channel_id=1, source_target_pairs={{0,32},{16,48},{32,0},{48,16},{1,33},{17,49},{33,1},{49,17},{2,34}... | collective-permute-start | bytes 98312 | tf_op jit(solution)/shard_map/ppermute | solution.py:146
  31.2 1.1 %collective-permute-start.9 = (bf16[128,128]{1,0:T(8,128)(2,1)S(1)}, bf16[128,128]{1,0:T(8,128)(2,1)S(1)}, u32[]{:S(2)}, u32[]{:S(2)}) collective-permute-start(bf16[128,128]{1,0:T(8,128)(2,1)S(1)} %get-tuple-element.19.q0), channel_id=1, source_target_pairs={{0,48},{16,0},{32,16},{48,32},{1,49},{17,1},{33,17},{49,33},{2,50}... | collective-permute-start | bytes 98312 | tf_op jit(solution)/shard_map/ppermute | solution.py:146
  32.3 0.0 collective-permute-done.7.q1
  32.3 0.8 %collective-permute-done.8.q2 = bf16[128,128]{1,0:T(8,128)(2,1)S(1)} collective-permute-done((bf16[128,128]{1,0:T(8,128)(2,1)S(1)}, bf16[128,128]{1,0:T(8,128)(2,1)S(1)}, u32[]{:S(2)}, u32[]{:S(2)}) %collective-permute-start.8) | collective-permute-done | bytes 32800 | tf_op jit(solution)/shard_map/ppermute | solution.py:146
  33.1 1.2 %collective-permute-done.9.q3 = bf16[128,128]{1,0:T(8,128)(2,1)S(1)} collective-permute-done((bf16[128,128]{1,0:T(8,128)(2,1)S(1)}, bf16[128,128]{1,0:T(8,128)(2,1)S(1)}, u32[]{:S(2)}, u32[]{:S(2)}) %collective-permute-start.9) | collective-permute-done | bytes 32800 | tf_op jit(solution)/shard_map/ppermute | solution.py:146
  34.2 0.6 %all-to-all-done.train = bf16[16,32,128]{2,1,0:T(8,128)(2,1)S(1)} async-done(((bf16[16,32,128]{2,1,0:T(8,128)(2,1)}), bf16[16,32,128]{2,1,0:T(8,128)(2,1)S(1)}, u32[]{:S(2)}, u32[]{:S(2)}) %all-to-all-start) | async-done | bytes 131104 | tf_op jit(solution)/shard_map/all_to_all | solution.py:218
  34.9 0.8 %score.1 = f32[64,128]{1,0:T(8,128)S(1)} custom-call(bf16[16,32,128]{2,1,0:T(8,128)(2,1)S(1)} %all-to-all-done.train, bf16[128,128]{1,0:T(8,128)(2,1)S(1)} %get-tuple-element.19.q0, bf16[128,128]{1,0:T(8,128)(2,1)S(1)} %collective-permute-done.7.q1, bf16[128,128]{1,0:T(8,128)(2,1)S(1)} %collective-permute-done.8.q2, ...), custom_call_target="tpu_custom_call" | custom-call | tf_op jit(solution)/shard_map/score/pallas_call | solution.py:219
  35.7 23.8 %all_to_all.10 = f32[64,1,128]{2,1,0:T(1,128)S(1)} all-to-all(f32[64,1,128]{2,1,0:T(1,128)S(1)} %bitcast.23), channel_id=1, replica_groups=mesh['z_hi'=2,'core'=2,'y'=4,'x'=4,'z_lo'=4] {'z_hi','core','x','z_lo'}, dimensions={0} | all-to-all | bytes 65536 | tf_op jit(solution)/shard_map/all_to_all | solution.py:228
  59.5 0.6 reduce_sum.11
Async XLA Ops:
  0.0 9.4 %collective-permute-start.3 = (bf16[128,4096]{1,0:T(8,128)(2,1)}, bf16[128,4096]{1,0:T(8,128)(2,1)S(1)}, u32[]{:S(2)}, u32[]{:S(2)}) collective-permute-start(bf16[128,4096]{1,0:T(8,128)(2,1)} %bitcast.16), channel_id=1, source_target_pairs={{0,64},{64,0},{1,65},{65,1},{2,66},{66,2},{3,67},{67,3},{4,68},{68... | collective-permute-start | bytes 3145736 | tf_op jit(solution)/shard_map/ppermute | solution.py:142
  3.2 6.1 %collective-permute-start.4 = (bf16[128,4096]{1,0:T(8,128)(2,1)}, bf16[128,4096]{1,0:T(8,128)(2,1)S(1)}, u32[]{:S(2)}, u32[]{:S(2)}) collective-permute-start(bf16[128,4096]{1,0:T(8,128)(2,1)} %bitcast.18), channel_id=1, source_target_pairs={{0,64},{64,0},{1,65},{65,1},{2,66},{66,2},{3,67},{67,3},{4,68},{68... | collective-permute-start | bytes 3145736 | tf_op jit(solution)/shard_map/ppermute | solution.py:142
  3.2 6.1 %copy-start = (bf16[1,128,4096]{2,1,0:T(8,128)(2,1)S(1)}, bf16[1,128,4096]{2,1,0:T(8,128)(2,1)}, u32[]{:S(2)}) copy-start(bf16[1,128,4096]{2,1,0:T(8,128)(2,1)} %param.12) | copy-start | bytes 3145732
  3.2 6.2 %copy-start.1 = (bf16[1,128,4096]{2,1,0:T(8,128)(2,1)S(1)}, bf16[1,128,4096]{2,1,0:T(8,128)(2,1)}, u32[]{:S(2)}) copy-start(bf16[1,128,4096]{2,1,0:T(8,128)(2,1)} %param.14) | copy-start | bytes 3145732
  3.2 6.2 %copy-start.2 = (bf16[1,128,4096]{2,1,0:T(8,128)(2,1)S(1)}, bf16[1,128,4096]{2,1,0:T(8,128)(2,1)}, u32[]{:S(2)}) copy-start(bf16[1,128,4096]{2,1,0:T(8,128)(2,1)} %param.13) | copy-start | bytes 3145732
  3.3 6.2 %copy-start.3 = (bf16[1,128,4096]{2,1,0:T(8,128)(2,1)S(1)}, bf16[1,128,4096]{2,1,0:T(8,128)(2,1)}, u32[]{:S(2)}) copy-start(bf16[1,128,4096]{2,1,0:T(8,128)(2,1)} %param.15) | copy-start | bytes 3145732
  3.3 6.2 %copy-start.4 = (bf16[1,4096,64]{1,2,0:T(8,128)(2,1)S(1)}, bf16[1,4096,64]{1,2,0:T(8,128)(2,1)}, u32[]{:S(2)}) copy-start(bf16[1,4096,64]{1,2,0:T(8,128)(2,1)} %param.16) | copy-start | bytes 1572868
  3.3 6.2 %copy-start.5 = (bf16[1,4096,64]{1,2,0:T(8,128)(2,1)S(1)}, bf16[1,4096,64]{1,2,0:T(8,128)(2,1)}, u32[]{:S(2)}) copy-start(bf16[1,4096,64]{1,2,0:T(8,128)(2,1)} %param.17) | copy-start | bytes 1572868
  3.3 6.2 %copy-start.6 = (s32[8,16]{1,0:T(8,128)S(1)}, s32[8,16]{1,0:T(8,128)}, u32[]{:S(2)}) copy-start(s32[8,16]{1,0:T(8,128)} %query_ids.1) | copy-start | bytes 1540
  3.3 6.2 %copy-start.7 = (s32[1,128]{1,0:T(1,128)S(1)}, s32[1,128]{1,0:T(1,128)}, u32[]{:S(2)}) copy-start(s32[1,128]{1,0:T(1,128)} %train_ids.1) | copy-start | bytes 1540
  4.4 10.1 %collective-permute-start.5 = (bf16[16,4096]{1,0:T(8,128)(2,1)S(1)}, bf16[16,4096]{1,0:T(8,128)(2,1)S(1)}, u32[]{:S(2)}, u32[]{:S(2)}) collective-permute-start(bf16[16,4096]{1,0:T(8,128)(2,1)S(1)} %send.1), channel_id=1, source_target_pairs={{0,131},{1,130},{2,129},{3,128},{4,135},{5,134},{6,133},{7,132},{8... | collective-permute-start | bytes 393224 | tf_op jit(solution)/shard_map/ppermute | solution.py:186
  11.4 9.8 %collective-permute-start.6 = (bf16[4,64,128]{2,1,0:T(8,128)(2,1)S(1)}, bf16[4,64,128]{2,1,0:T(8,128)(2,1)S(1)}, u32[]{:S(2)}, u32[]{:S(2)}) collective-permute-start(bf16[4,64,128]{2,1,0:T(8,128)(2,1)S(1)} %get-tuple-element.17), channel_id=1, source_target_pairs={{0,128},{128,0},{1,129},{129,1},{2,130},{130,2},{3,131},{131,3},{4... | collective-permute-start | bytes 196616 | tf_op jit(solution)/shard_map/ppermute | solution.py:142
  14.5 5.3 %collective-permute-start = (bf16[16,4096]{1,0:T(8,128)(2,1)S(1)}, bf16[16,4096]{1,0:T(8,128)(2,1)}, u32[]{:S(2)}, u32[]{:S(2)}) collective-permute-start(bf16[16,4096]{1,0:T(8,128)(2,1)S(1)} %param.1), channel_id=1, source_target_pairs={{0,4},{4,8},{8,12},{12,0},{1,5},{5,9},{9,13},{13,1},{2,6},{6,10},{... | collective-permute-start | bytes 393224 | tf_op jit(solution)/shard_map/cond/branch_1_fun/ppermute | solution.py:146
  15.7 5.5 %collective-permute-start.1 = (bf16[16,4096]{1,0:T(8,128)(2,1)S(1)}, bf16[16,4096]{1,0:T(8,128)(2,1)}, u32[]{:S(2)}, u32[]{:S(2)}) collective-permute-start(bf16[16,4096]{1,0:T(8,128)(2,1)S(1)} %param.1), channel_id=1, source_target_pairs={{0,16},{16,32},{32,48},{48,0},{1,17},{17,33},{33,49},{49,1},{2,18}... | collective-permute-start | bytes 393224 | tf_op jit(solution)/shard_map/cond/branch_1_fun/ppermute | solution.py:146
  17.0 4.2 %collective-permute-start.2 = (bf16[16,4096]{1,0:T(8,128)(2,1)S(1)}, bf16[16,4096]{1,0:T(8,128)(2,1)}, u32[]{:S(2)}, u32[]{:S(2)}) collective-permute-start(bf16[16,4096]{1,0:T(8,128)(2,1)S(1)} %param.1), channel_id=1, source_target_pairs={{0,12},{4,0},{8,4},{12,8},{1,13},{5,1},{9,5},{13,9},{2,14},{6,2},{... | collective-permute-start | bytes 393224 | tf_op jit(solution)/shard_map/cond/branch_1_fun/ppermute | solution.py:146
  22.2 12.7 %all-to-all-start = ((bf16[16,32,128]{2,1,0:T(8,128)(2,1)}), bf16[16,32,128]{2,1,0:T(8,128)(2,1)S(1)}, u32[]{:S(2)}, u32[]{:S(2)}) async-start(bf16[16,32,128]{2,1,0:T(8,128)(2,1)} %get-tuple-element.18), calls=%async_computation | async-start | bytes 262144 | tf_op jit(solution)/shard_map/all_to_all | solution.py:218
  27.6 4.7 %collective-permute-start.7 = (bf16[128,128]{1,0:T(8,128)(2,1)S(1)}, bf16[128,128]{1,0:T(8,128)(2,1)S(1)}, u32[]{:S(2)}, u32[]{:S(2)}) collective-permute-start(bf16[128,128]{1,0:T(8,128)(2,1)S(1)} %get-tuple-element.19.q0), channel_id=1, source_target_pairs={{0,16},{16,32},{32,48},{48,0},{1,17},{17,33},{33,49},{49,1},{2,18}... | collective-permute-start | bytes 98312 | tf_op jit(solution)/shard_map/ppermute | solution.py:146
  28.8 4.3 %collective-permute-start.8 = (bf16[128,128]{1,0:T(8,128)(2,1)S(1)}, bf16[128,128]{1,0:T(8,128)(2,1)S(1)}, u32[]{:S(2)}, u32[]{:S(2)}) collective-permute-start(bf16[128,128]{1,0:T(8,128)(2,1)S(1)} %get-tuple-element.19.q0), channel_id=1, source_target_pairs={{0,32},{16,48},{32,0},{48,16},{1,33},{17,49},{33,1},{49,17},{2,34}... | collective-permute-start | bytes 98312 | tf_op jit(solution)/shard_map/ppermute | solution.py:146
  31.2 3.0 %collective-permute-start.9 = (bf16[128,128]{1,0:T(8,128)(2,1)S(1)}, bf16[128,128]{1,0:T(8,128)(2,1)S(1)}, u32[]{:S(2)}, u32[]{:S(2)}) collective-permute-start(bf16[128,128]{1,0:T(8,128)(2,1)S(1)} %get-tuple-element.19.q0), channel_id=1, source_target_pairs={{0,48},{16,0},{32,16},{48,32},{1,49},{17,1},{33,17},{49,33},{2,50}... | collective-permute-start | bytes 98312 | tf_op jit(solution)/shard_map/ppermute | solution.py:146
where the time goes:
time: 60.4 us; the launch traced here: 60.1 us
  starting transfers between devices  25.4 us (42%)
  blocking collectives  23.8 us (39%)
  waiting for transfers between devices  5.36 us (9%)
  Pallas kernels  4.8 us (8%)
    all_to_all x1, blocking collectives, on_device(): landed = lax.all_to_all(terms.reshape(64, 1, 128), LAYER + PLANE, 0, 0)  23.8 us
    ppermute x6, starting transfers between devices, shift(): return lax.ppermute(value, axis, [(i, (i + k) % 4) for i in range(4)])  8.63 us
    ppermute x3, starting transfers between devices, swap(): return lambda value: lax.ppermute(value, axis, [(0, 1), (1, 0)])  6.32 us
    all_to_all x1, starting transfers between devices, on_device(): trains = lax.all_to_all(train, PLANE, 0, 0)  5.43 us
    ppermute x1, starting transfers between devices, on_device(): w0 = lax.ppermute(mine, ('z_hi', 'z_lo'), [(k, 7 - k) for k in range(4)])  4.96 us
    ppermute x6, waiting for transfers between devices, shift(): return lax.ppermute(value, axis, [(i, (i + k) % 4) for i in range(4)])  4.72 us
    pallas_call x1, Pallas kernels, on_device(): pl.pallas_call(own_kernel, out_shape=(jax.ShapeDtypeStruct((4, K_OUT, 128...  1.97 us
  transfers between devices with their start and end apart: 11, of which 5 were waited for; matrix products, arithmetic and copies ran while one was open for 0% of the time, Pallas kernels for 3%

commit v1 on v0

--- a/solution.py
+++ b/solution.py
@@ -66,6 +66,10 @@
         move = pltpu.make_async_copy(wo.at[pl.ds(at, ROWS)], mine, sem)
         move.start()
         move.wait()
+
+    @pl.when(lax.axis_index("z_hi") == 1)
+    def _():
+        mine[...] = jnp.zeros_like(mine)
 
 
 def own_kernel(train_ids, query_ids, ta, qa, tc, qc, tb, qb, wi, wo, held, total, chosen):
@@ -183,7 +187,7 @@
         cost_estimate=pl.CostEstimate(flops=20000000000, bytes_accessed=1 << 20, transcendentals=0),
         name="send",
     )(wo)
-    w0 = lax.ppermute(mine, ("z_hi", "z_lo"), [(k, 7 - k) for k in range(4)])
+    w0 = lax.ppermute(mine, ("z_hi", "z_lo"), [(k, 7 - k) for k in range(8)])
     held, total = pl.pallas_call(
         own_kernel,
         out_shape=(

time: 60.4 us -> 58.3 us (0.965)
  blocking collectives: 23.8 us -> 21.7 us
    ppermute x3, starting transfers between devices: 6.32 us -> 8.43 us  [swap(): return lambda value: lax.ppermute(value, axis, [(0, 1), (1, 0)])]
    ppermute x1, starting transfers between devices: 4.96 us -> 2.88 us  [on_device(): w0 = lax.ppermute(mine, ('z_hi', 'z_lo'), [(k, 7 - k) for k in range(8)])]
    all_to_all x1, blocking collectives: 23.8 us -> 21.7 us  [on_device(): landed = lax.all_to_all(terms.reshape(64, 1, 128), LAYER + PLANE, 0, 0)]
    all_to_all x1, waiting for transfers between devices: 0.64 us -> 1.68 us  [on_device(): trains = lax.all_to_all(train, PLANE, 0, 0)]
    ppermute x6, waiting for transfers between devices: 4.72 us -> 3.78 us  [shift(): return lax.ppermute(value, axis, [(i, (i + k) % 4) for i in range(4)])]
where the time goes in v1:
time: 58.3 us; the launch traced here: 58.1 us
  starting transfers between devices  25.3 us (43%)
  blocking collectives  21.7 us (37%)
  waiting for transfers between devices  5.46 us (9%)
  Pallas kernels  4.8 us (8%)
  other arithmetic  0.59 us (1%)
    all_to_all x1, blocking collectives, on_device(): landed = lax.all_to_all(terms.reshape(64, 1, 128), LAYER + PLANE, 0, 0)  21.7 us
    ppermute x6, starting transfers between devices, shift(): return lax.ppermute(value, axis, [(i, (i + k) % 4) for i in range(4)])  8.53 us
    ppermute x3, starting transfers between devices, swap(): return lambda value: lax.ppermute(value, axis, [(0, 1), (1, 0)])  8.43 us
    all_to_all x1, starting transfers between devices, on_device(): trains = lax.all_to_all(train, PLANE, 0, 0)  5.43 us
    ppermute x6, waiting for transfers between devices, shift(): return lax.ppermute(value, axis, [(i, (i + k) % 4) for i in range(4)])  3.78 us
    ppermute x1, starting transfers between devices, on_device(): w0 = lax.ppermute(mine, ('z_hi', 'z_lo'), [(k, 7 - k) for k in range(8)])  2.88 us
    pallas_call x1, Pallas kernels, on_device(): pl.pallas_call(own_kernel, out_shape=(jax.ShapeDtypeStruct((4, K_OUT, 128...  1.96 us
    all_to_all x1, waiting for transfers between devices, on_device(): trains = lax.all_to_all(train, PLANE, 0, 0)  1.68 us
  transfers between devices with their start and end apart: 11, of which 5 were waited for; matrix products, arithmetic and copies ran while one was open for 0% of the time, Pallas kernels for 3%

profile of v1, /device:TPU:1, one launch (start us, length us, event | category | flops | bytes accessed | tf_op | source)
XLA Modules:
  0.0 58.1 jit_solution(2483808971221708695)
XLA Ops:
  0.0 3.2 %collective-permute-start.3 = (bf16[128,4096]{1,0:T(8,128)(2,1)}, bf16[128,4096]{1,0:T(8,128)(2,1)S(1)}, u32[]{:S(2)}, u32[]{:S(2)}) collective-permute-start(bf16[128,4096]{1,0:T(8,128)(2,1)} %bitcast.16), channel_id=1, source_target_pairs={{0,64},{64,0},{1,65},{65,1},{2,66},{66,2},{3,67},{67,3},{4,68},{68... | collective-permute-start | bytes 3145736 | tf_op jit(solution)/shard_map/ppermute | solution.py:146
  3.2 0.0 collective-permute-start.4
  3.2 0.0 copy-start
  3.2 0.0 copy-start.1
  3.2 0.0 copy-start.2
  3.3 0.0 copy-start.3
  3.3 0.0 copy-start.4
  3.3 0.0 copy-start.5
  3.3 0.0 copy-start.6
  3.3 0.0 copy-start.7
  3.3 1.1 %send.1 = bf16[16,4096]{1,0:T(8,128)(2,1)S(1)} custom-call(bf16[64,4096]{1,0:T(8,128)(2,1)} %bitcast.21), custom_call_target="tpu_custom_call" | custom-call | flops 20000000000 | bytes 1048576 | tf_op jit(solution)/shard_map/send/pallas_call | solution.py:180
  4.4 2.9 %collective-permute-start.5 = (bf16[16,4096]{1,0:T(8,128)(2,1)S(1)}, bf16[16,4096]{1,0:T(8,128)(2,1)S(1)}, u32[]{:S(2)}, u32[]{:S(2)}) collective-permute-start(bf16[16,4096]{1,0:T(8,128)(2,1)S(1)} %send.1), channel_id=1, source_target_pairs={{0,131},{1,130},{2,129},{3,128},{128,3},{129,2},{130,1},{131,0},{4... | collective-permute-start | bytes 393224 | tf_op jit(solution)/shard_map/ppermute | solution.py:190
  7.3 0.0 collective-permute-done.3.tb
  7.3 0.0 collective-permute-done.4.qb
  7.3 0.0 copy-done
  7.3 0.0 copy-done.1
  7.3 0.0 copy-done.2
  7.3 0.0 copy-done.3
  7.3 0.0 copy-done.4
  7.3 0.0 copy-done.5
  7.3 0.0 copy-done.6
  7.4 0.0 copy-done.7
  7.4 2.0 %own.1 = (bf16[4,64,128]{2,1,0:T(8,128)(2,1)S(1)}, bf16[256,4096]{1,0:T(8,128)(2,1)S(1)}) custom-call(s32[1,128]{1,0:T(1,128)S(1)} %copy-done.7, s32[8,16]{1,0:T(8,128)S(1)} %copy-done.6, bf16[128,4096]{1,0:T(8,128)(2,1)S(1)} %bitcast.14, bf16[128,4096]{1,0:T(8,128)(2,1)S(1)} %bitcast.15, bf16[128,4096]{1,0:T(8,128)(2,1)S(1)} %bitcast.17, ...), custom_call_target="tpu_custom_call" | custom-call | tf_op jit(solution)/shard_map/own/pallas_call | solution.py:191
  9.3 5.2 %collective-permute-start.6 = (bf16[4,64,128]{2,1,0:T(8,128)(2,1)S(1)}, bf16[4,64,128]{2,1,0:T(8,128)(2,1)S(1)}, u32[]{:S(2)}, u32[]{:S(2)}) collective-permute-start(bf16[4,64,128]{2,1,0:T(8,128)(2,1)S(1)} %get-tuple-element.17), channel_id=1, source_target_pairs={{0,128},{128,0},{1,129},{129,1},{2,130},{130,2},{3,131},{131,3},{4... | collective-permute-start | bytes 196616 | tf_op jit(solution)/shard_map/ppermute | solution.py:146
  14.5 0.0 collective-permute-done.5.w0
  14.5 6.7 %conditional.1 = (bf16[16,4096]{1,0:T(8,128)(2,1)}, bf16[16,4096]{1,0:T(8,128)(2,1)}, bf16[16,4096]{1,0:T(8,128)(2,1)}) conditional(s32[]{:T(128)} %convert_element_type.3, () %tuple.13, bf16[16,4096]{1,0:T(8,128)(2,1)S(1)} %collective-permute-done.5.w0), branch_computations={%region_0.0_spmd, %region_1.0_spmd} | conditional | bytes 1573008 | solution.py:159
  14.5 1.2 %collective-permute-start = (bf16[16,4096]{1,0:T(8,128)(2,1)S(1)}, bf16[16,4096]{1,0:T(8,128)(2,1)}, u32[]{:S(2)}, u32[]{:S(2)}) collective-permute-start(bf16[16,4096]{1,0:T(8,128)(2,1)S(1)} %param.1), channel_id=1, source_target_pairs={{0,4},{4,8},{8,12},{12,0},{1,5},{5,9},{9,13},{13,1},{2,6},{6,10},{... | collective-permute-start | bytes 393224 | tf_op jit(solution)/shard_map/cond/branch_1_fun/ppermute | solution.py:150
  15.7 1.3 %collective-permute-start.1 = (bf16[16,4096]{1,0:T(8,128)(2,1)S(1)}, bf16[16,4096]{1,0:T(8,128)(2,1)}, u32[]{:S(2)}, u32[]{:S(2)}) collective-permute-start(bf16[16,4096]{1,0:T(8,128)(2,1)S(1)} %param.1), channel_id=1, source_target_pairs={{0,16},{16,32},{32,48},{48,0},{1,17},{17,33},{33,49},{49,1},{2,18}... | collective-permute-start | bytes 393224 | tf_op jit(solution)/shard_map/cond/branch_1_fun/ppermute | solution.py:150
  17.0 1.5 %collective-permute-start.2 = (bf16[16,4096]{1,0:T(8,128)(2,1)S(1)}, bf16[16,4096]{1,0:T(8,128)(2,1)}, u32[]{:S(2)}, u32[]{:S(2)}) collective-permute-start(bf16[16,4096]{1,0:T(8,128)(2,1)S(1)} %param.1), channel_id=1, source_target_pairs={{0,12},{4,0},{8,4},{12,8},{1,13},{5,1},{9,5},{13,9},{2,14},{6,2},{... | collective-permute-start | bytes 393224 | tf_op jit(solution)/shard_map/cond/branch_1_fun/ppermute | solution.py:150
  18.5 1.7 %collective-permute-done = bf16[16,4096]{1,0:T(8,128)(2,1)} collective-permute-done((bf16[16,4096]{1,0:T(8,128)(2,1)S(1)}, bf16[16,4096]{1,0:T(8,128)(2,1)}, u32[]{:S(2)}, u32[]{:S(2)}) %collective-permute-start) | collective-permute-done | bytes 131104 | tf_op jit(solution)/shard_map/cond/branch_1_fun/ppermute | solution.py:150
  20.2 1.0 %collective-permute-done.1 = bf16[16,4096]{1,0:T(8,128)(2,1)} collective-permute-done((bf16[16,4096]{1,0:T(8,128)(2,1)S(1)}, bf16[16,4096]{1,0:T(8,128)(2,1)}, u32[]{:S(2)}, u32[]{:S(2)}) %collective-permute-start.1) | collective-permute-done | bytes 131104 | tf_op jit(solution)/shard_map/cond/branch_1_fun/ppermute | solution.py:150
  21.2 0.0 collective-permute-done.2
  21.3 0.0 collective-permute-done.6.got
  21.3 0.9 %pair.1 = (bf16[16,32,128]{2,1,0:T(8,128)(2,1)}, bf16[128,128]{1,0:T(8,128)(2,1)S(1)}) custom-call(bf16[256,4096]{1,0:T(8,128)(2,1)S(1)} %get-tuple-element.13.total, bf16[16,4096]{1,0:T(8,128)(2,1)S(1)} %collective-permute-done.5.w0, bf16[16,4096]{1,0:T(8,128)(2,1)} %get-tuple-element.14.w1, bf16[16,4096]{1,0:T(8,128)(2,1)} %get-tuple-element.15.w2, ...), custom_call_target="tpu_custom_call" | custom-call | tf_op jit(solution)/shard_map/pair/pallas_call | solution.py:205
  22.2 5.4 %all-to-all-start = ((bf16[16,32,128]{2,1,0:T(8,128)(2,1)}), bf16[16,32,128]{2,1,0:T(8,128)(2,1)S(1)}, u32[]{:S(2)}, u32[]{:S(2)}) async-start(bf16[16,32,128]{2,1,0:T(8,128)(2,1)} %get-tuple-element.18), calls=%async_computation | async-start | bytes 262144 | tf_op jit(solution)/shard_map/all_to_all | solution.py:222
  27.6 1.2 %collective-permute-start.7 = (bf16[128,128]{1,0:T(8,128)(2,1)S(1)}, bf16[128,128]{1,0:T(8,128)(2,1)S(1)}, u32[]{:S(2)}, u32[]{:S(2)}) collective-permute-start(bf16[128,128]{1,0:T(8,128)(2,1)S(1)} %get-tuple-element.19.q0), channel_id=1, source_target_pairs={{0,16},{16,32},{32,48},{48,0},{1,17},{17,33},{33,49},{49,1},{2,18}... | collective-permute-start | bytes 98312 | tf_op jit(solution)/shard_map/ppermute | solution.py:150
  28.8 1.4 %collective-permute-start.8 = (bf16[128,128]{1,0:T(8,128)(2,1)S(1)}, bf16[128,128]{1,0:T(8,128)(2,1)S(1)}, u32[]{:S(2)}, u32[]{:S(2)}) collective-permute-start(bf16[128,128]{1,0:T(8,128)(2,1)S(1)} %get-tuple-element.19.q0), channel_id=1, source_target_pairs={{0,32},{16,48},{32,0},{48,16},{1,33},{17,49},{33,1},{49,17},{2,34}... | collective-permute-start | bytes 98312 | tf_op jit(solution)/shard_map/ppermute | solution.py:150
  30.2 2.0 %collective-permute-start.9 = (bf16[128,128]{1,0:T(8,128)(2,1)S(1)}, bf16[128,128]{1,0:T(8,128)(2,1)S(1)}, u32[]{:S(2)}, u32[]{:S(2)}) collective-permute-start(bf16[128,128]{1,0:T(8,128)(2,1)S(1)} %get-tuple-element.19.q0), channel_id=1, source_target_pairs={{0,48},{16,0},{32,16},{48,32},{1,49},{17,1},{33,17},{49,33},{2,50}... | collective-permute-start | bytes 98312 | tf_op jit(solution)/shard_map/ppermute | solution.py:150
  32.2 0.0 collective-permute-done.7.q1
  32.2 0.9 %collective-permute-done.8.q2 = bf16[128,128]{1,0:T(8,128)(2,1)S(1)} collective-permute-done((bf16[128,128]{1,0:T(8,128)(2,1)S(1)}, bf16[128,128]{1,0:T(8,128)(2,1)S(1)}, u32[]{:S(2)}, u32[]{:S(2)}) %collective-permute-start.8) | collective-permute-done | bytes 32800 | tf_op jit(solution)/shard_map/ppermute | solution.py:150
  33.1 0.2 collective-permute-done.9.q3
  33.2 1.7 %all-to-all-done.train = bf16[16,32,128]{2,1,0:T(8,128)(2,1)S(1)} async-done(((bf16[16,32,128]{2,1,0:T(8,128)(2,1)}), bf16[16,32,128]{2,1,0:T(8,128)(2,1)S(1)}, u32[]{:S(2)}, u32[]{:S(2)}) %all-to-all-start) | async-done | bytes 131104 | tf_op jit(solution)/shard_map/all_to_all | solution.py:222
  34.9 0.8 %score.1 = f32[64,128]{1,0:T(8,128)S(1)} custom-call(bf16[16,32,128]{2,1,0:T(8,128)(2,1)S(1)} %all-to-all-done.train, bf16[128,128]{1,0:T(8,128)(2,1)S(1)} %get-tuple-element.19.q0, bf16[128,128]{1,0:T(8,128)(2,1)S(1)} %collective-permute-done.7.q1, bf16[128,128]{1,0:T(8,128)(2,1)S(1)} %collective-permute-done.8.q2, ...), custom_call_target="tpu_custom_call" | custom-call | tf_op jit(solution)/shard_map/score/pallas_call | solution.py:223
  35.7 21.7 %all_to_all.10 = f32[64,1,128]{2,1,0:T(1,128)S(1)} all-to-all(f32[64,1,128]{2,1,0:T(1,128)S(1)} %bitcast.23), channel_id=1, replica_groups=mesh['z_hi'=2,'core'=2,'y'=4,'x'=4,'z_lo'=4] {'z_hi','core','x','z_lo'}, dimensions={0} | all-to-all | bytes 65536 | tf_op jit(solution)/shard_map/all_to_all | solution.py:232
  57.5 0.6 %reduce_sum.11 = f32[128]{0:T(128)} reduce(f32[64,1,128]{2,1,0:T(1,128)S(1)} %all_to_all.10, f32[]{:T(128)} %constant.11.clone.1), dimensions={0,1}, to_apply=%region_2.0 | reduce | flops 8064 | bytes 33284 | tf_op jit(solution)/shard_map/reduce_sum | solution.py:233
Async XLA Ops:
  0.0 7.3 %collective-permute-start.3 = (bf16[128,4096]{1,0:T(8,128)(2,1)}, bf16[128,4096]{1,0:T(8,128)(2,1)S(1)}, u32[]{:S(2)}, u32[]{:S(2)}) collective-permute-start(bf16[128,4096]{1,0:T(8,128)(2,1)} %bitcast.16), channel_id=1, source_target_pairs={{0,64},{64,0},{1,65},{65,1},{2,66},{66,2},{3,67},{67,3},{4,68},{68... | collective-permute-start | bytes 3145736 | tf_op jit(solution)/shard_map/ppermute | solution.py:146
  3.2 4.0 %collective-permute-start.4 = (bf16[128,4096]{1,0:T(8,128)(2,1)}, bf16[128,4096]{1,0:T(8,128)(2,1)S(1)}, u32[]{:S(2)}, u32[]{:S(2)}) collective-permute-start(bf16[128,4096]{1,0:T(8,128)(2,1)} %bitcast.18), channel_id=1, source_target_pairs={{0,64},{64,0},{1,65},{65,1},{2,66},{66,2},{3,67},{67,3},{4,68},{68... | collective-permute-start | bytes 3145736 | tf_op jit(solution)/shard_map/ppermute | solution.py:146
  3.2 4.0 %copy-start = (bf16[1,128,4096]{2,1,0:T(8,128)(2,1)S(1)}, bf16[1,128,4096]{2,1,0:T(8,128)(2,1)}, u32[]{:S(2)}) copy-start(bf16[1,128,4096]{2,1,0:T(8,128)(2,1)} %param.12) | copy-start | bytes 3145732
  3.2 4.0 %copy-start.1 = (bf16[1,128,4096]{2,1,0:T(8,128)(2,1)S(1)}, bf16[1,128,4096]{2,1,0:T(8,128)(2,1)}, u32[]{:S(2)}) copy-start(bf16[1,128,4096]{2,1,0:T(8,128)(2,1)} %param.14) | copy-start | bytes 3145732
  3.2 4.1 %copy-start.2 = (bf16[1,128,4096]{2,1,0:T(8,128)(2,1)S(1)}, bf16[1,128,4096]{2,1,0:T(8,128)(2,1)}, u32[]{:S(2)}) copy-start(bf16[1,128,4096]{2,1,0:T(8,128)(2,1)} %param.13) | copy-start | bytes 3145732
  3.3 4.1 %copy-start.3 = (bf16[1,128,4096]{2,1,0:T(8,128)(2,1)S(1)}, bf16[1,128,4096]{2,1,0:T(8,128)(2,1)}, u32[]{:S(2)}) copy-start(bf16[1,128,4096]{2,1,0:T(8,128)(2,1)} %param.15) | copy-start | bytes 3145732
  3.3 4.1 %copy-start.4 = (bf16[1,4096,64]{1,2,0:T(8,128)(2,1)S(1)}, bf16[1,4096,64]{1,2,0:T(8,128)(2,1)}, u32[]{:S(2)}) copy-start(bf16[1,4096,64]{1,2,0:T(8,128)(2,1)} %param.16) | copy-start | bytes 1572868
  3.3 4.1 %copy-start.5 = (bf16[1,4096,64]{1,2,0:T(8,128)(2,1)S(1)}, bf16[1,4096,64]{1,2,0:T(8,128)(2,1)}, u32[]{:S(2)}) copy-start(bf16[1,4096,64]{1,2,0:T(8,128)(2,1)} %param.17) | copy-start | bytes 1572868
  3.3 4.1 %copy-start.6 = (s32[8,16]{1,0:T(8,128)S(1)}, s32[8,16]{1,0:T(8,128)}, u32[]{:S(2)}) copy-start(s32[8,16]{1,0:T(8,128)} %query_ids.1) | copy-start | bytes 1540
  3.3 4.1 %copy-start.7 = (s32[1,128]{1,0:T(1,128)S(1)}, s32[1,128]{1,0:T(1,128)}, u32[]{:S(2)}) copy-start(s32[1,128]{1,0:T(1,128)} %train_ids.1) | copy-start | bytes 1540
  4.4 10.1 %collective-permute-start.5 = (bf16[16,4096]{1,0:T(8,128)(2,1)S(1)}, bf16[16,4096]{1,0:T(8,128)(2,1)S(1)}, u32[]{:S(2)}, u32[]{:S(2)}) collective-permute-start(bf16[16,4096]{1,0:T(8,128)(2,1)S(1)} %send.1), channel_id=1, source_target_pairs={{0,131},{1,130},{2,129},{3,128},{128,3},{129,2},{130,1},{131,0},{4... | collective-permute-start | bytes 393224 | tf_op jit(solution)/shard_map/ppermute | solution.py:190
  9.3 11.9 %collective-permute-start.6 = (bf16[4,64,128]{2,1,0:T(8,128)(2,1)S(1)}, bf16[4,64,128]{2,1,0:T(8,128)(2,1)S(1)}, u32[]{:S(2)}, u32[]{:S(2)}) collective-permute-start(bf16[4,64,128]{2,1,0:T(8,128)(2,1)S(1)} %get-tuple-element.17), channel_id=1, source_target_pairs={{0,128},{128,0},{1,129},{129,1},{2,130},{130,2},{3,131},{131,3},{4... | collective-permute-start | bytes 196616 | tf_op jit(solution)/shard_map/ppermute | solution.py:146
  14.5 5.7 %collective-permute-start = (bf16[16,4096]{1,0:T(8,128)(2,1)S(1)}, bf16[16,4096]{1,0:T(8,128)(2,1)}, u32[]{:S(2)}, u32[]{:S(2)}) collective-permute-start(bf16[16,4096]{1,0:T(8,128)(2,1)S(1)} %param.1), channel_id=1, source_target_pairs={{0,4},{4,8},{8,12},{12,0},{1,5},{5,9},{9,13},{13,1},{2,6},{6,10},{... | collective-permute-start | bytes 393224 | tf_op jit(solution)/shard_map/cond/branch_1_fun/ppermute | solution.py:150
  15.7 5.5 %collective-permute-start.1 = (bf16[16,4096]{1,0:T(8,128)(2,1)S(1)}, bf16[16,4096]{1,0:T(8,128)(2,1)}, u32[]{:S(2)}, u32[]{:S(2)}) collective-permute-start(bf16[16,4096]{1,0:T(8,128)(2,1)S(1)} %param.1), channel_id=1, source_target_pairs={{0,16},{16,32},{32,48},{48,0},{1,17},{17,33},{33,49},{49,1},{2,18}... | collective-permute-start | bytes 393224 | tf_op jit(solution)/shard_map/cond/branch_1_fun/ppermute | solution.py:150
  17.0 4.2 %collective-permute-start.2 = (bf16[16,4096]{1,0:T(8,128)(2,1)S(1)}, bf16[16,4096]{1,0:T(8,128)(2,1)}, u32[]{:S(2)}, u32[]{:S(2)}) collective-permute-start(bf16[16,4096]{1,0:T(8,128)(2,1)S(1)} %param.1), channel_id=1, source_target_pairs={{0,12},{4,0},{8,4},{12,8},{1,13},{5,1},{9,5},{13,9},{2,14},{6,2},{... | collective-permute-start | bytes 393224 | tf_op jit(solution)/shard_map/cond/branch_1_fun/ppermute | solution.py:150
  22.2 12.7 %all-to-all-start = ((bf16[16,32,128]{2,1,0:T(8,128)(2,1)}), bf16[16,32,128]{2,1,0:T(8,128)(2,1)S(1)}, u32[]{:S(2)}, u32[]{:S(2)}) async-start(bf16[16,32,128]{2,1,0:T(8,128)(2,1)} %get-tuple-element.18), calls=%async_computation | async-start | bytes 262144 | tf_op jit(solution)/shard_map/all_to_all | solution.py:222
  27.6 4.6 %collective-permute-start.7 = (bf16[128,128]{1,0:T(8,128)(2,1)S(1)}, bf16[128,128]{1,0:T(8,128)(2,1)S(1)}, u32[]{:S(2)}, u32[]{:S(2)}) collective-permute-start(bf16[128,128]{1,0:T(8,128)(2,1)S(1)} %get-tuple-element.19.q0), channel_id=1, source_target_pairs={{0,16},{16,32},{32,48},{48,0},{1,17},{17,33},{33,49},{49,1},{2,18}... | collective-permute-start | bytes 98312 | tf_op jit(solution)/shard_map/ppermute | solution.py:150
  28.8 4.3 %collective-permute-start.8 = (bf16[128,128]{1,0:T(8,128)(2,1)S(1)}, bf16[128,128]{1,0:T(8,128)(2,1)S(1)}, u32[]{:S(2)}, u32[]{:S(2)}) collective-permute-start(bf16[128,128]{1,0:T(8,128)(2,1)S(1)} %get-tuple-element.19.q0), channel_id=1, source_target_pairs={{0,32},{16,48},{32,0},{48,16},{1,33},{17,49},{33,1},{49,17},{2,34}... | collective-permute-start | bytes 98312 | tf_op jit(solution)/shard_map/ppermute | solution.py:150
  30.2 3.0 %collective-permute-start.9 = (bf16[128,128]{1,0:T(8,128)(2,1)S(1)}, bf16[128,128]{1,0:T(8,128)(2,1)S(1)}, u32[]{:S(2)}, u32[]{:S(2)}) collective-permute-start(bf16[128,128]{1,0:T(8,128)(2,1)S(1)} %get-tuple-element.19.q0), channel_id=1, source_target_pairs={{0,48},{16,0},{32,16},{48,32},{1,49},{17,1},{33,17},{49,33},{2,50}... | collective-permute-start | bytes 98312 | tf_op jit(solution)/shard_map/ppermute | solution.py:150
